TPU v7x, 256 devices: a whole 4x4x8 slice. The times are simulated.
256 devices in a mesh: lon: 32 (over z, x_lo, core), lat: 8 (over y, x_hi).
Axes of the slice: x: 4 (x_hi: 2, x_lo: 2; x = x_hi * 2 + x_lo), y: 4, z: 8, core: 2. Of those that a mesh axis runs over, the one named last changes fastest.
Arguments:
- tokens: bfloat16 [3, 192, 384, 512], P(None, 'lat', 'lon'), may hold values from -6 to 6
- valid: int32 [192, 384], replicated, may hold values 0 or 1
- w_qkv1: bfloat16 [512, 1536], P('lon'), may hold values from -0.25 to 0.25
- w_out1: bfloat16 [512, 512], P('lon'), may hold values from -0.25 to 0.25
- w_merge: bfloat16 [2048, 1024], P('lon'), may hold values from -0.125 to 0.125
- w_qkv2: bfloat16 [1024, 3072], P('lon'), may hold values from -0.1875 to 0.1875
- w_out2: bfloat16 [1024, 1024], P('lon'), may hold values from -0.1875 to 0.1875
- w_up: bfloat16 [1024, 2048], P('lon'), may hold values from -0.1875 to 0.1875
- gain1: float32 [512], replicated, may hold values from 0.5 to 2
- gain_merge: float32 [2048], replicated, may hold values from 0.5 to 2
- gain2: float32 [1024], replicated, may hold values from 0.5 to 2
- gain_up: float32 [512], replicated, may hold values from 0.5 to 2
- out_cot: bfloat16 [3, 192, 384, 512], P(None, 'lat', 'lon'), may hold values from -6 to 6
Outputs:
- output: bfloat16 [3, 192, 384, 512], P(None, 'lat', 'lon')
- grad_tokens: bfloat16 [3, 192, 384, 512], P(None, 'lat', 'lon')
All inputs are finite; a program needn't handle non-finite values.
Results may differ from a plain program's by a relative error of at most 0.039.
Values may be sent and summed in bfloat16 or wider, within the bound.
A program may use at most 192 MiB of HBM per device.

v0:
```python
import functools

import jax
import jax.numpy as jnp
import numpy as np
from jax import lax
from jax.experimental import pallas as pl
from jax.experimental.pallas import tpu as pltpu
from jax.sharding import PartitionSpec as P

EPS = 1e-05
BF = jnp.bfloat16
F32 = jnp.float32
LONS = 32
MIB = 1024 * 1024

PACK = {
    "qkv2": (0, 32, 24),
    "out2": (768, 32, 8),
    "merge": (1024, 64, 8),
    "up": (1536, 32, 16),
    "out1": (2048, 16, 4),
    "qkv1": (2112, 16, 12),
}
PACK_ROWS = 2304
SCALE = 32.0**-0.5
LOG2E = 1.4426950408889634
BLOCKED = -1e30


def permutations():
    merge_of_raw = np.zeros((512, 576), np.float32)
    quarter_of_raw = np.zeros((512, 576), np.float32)
    quarter_of_merge = np.zeros((128, 128), np.float32)
    for level in range(3):
        for row in range(6):
            for column in range(6):
                member = (row % 2) * 2 + column % 2
                merge_at = member * 32 + level * 9 + (row // 2) * 3 + column // 2
                quarter = (row // 3) * 2 + column // 3
                quarter_at = quarter * 32 + level * 9 + (row % 3) * 3 + column % 3
                quarter_of_merge[quarter_at, merge_at] = 1
                for band in range(4):
                    raw_at = level * 192 + column * 32 + band * 6 + row
                    merge_of_raw[band * 128 + merge_at, raw_at] = 1
                    quarter_of_raw[band * 128 + quarter_at, raw_at] = 1
    return merge_of_raw, quarter_of_raw, quarter_of_merge


def nn(a, b):
    return lax.dot_general(a, b, (((1,), (0,)), ((), ())), preferred_element_type=F32)


def nt(a, b):
    return lax.dot_general(a, b, (((1,), (1,)), ((), ())), preferred_element_type=F32)


def tn(a, b):
    return lax.dot_general(a, b, (((0,), (0,)), ((), ())), preferred_element_type=F32)


def weight_columns(ref, rows, tile, count):
    parts = []
    for step in range(count):
        start = pl.multiple_of((tile + step) * rows, rows)
        parts.append(ref[:, pl.ds(start, rows), :].reshape(LONS * rows, 128))
    return jnp.concatenate(parts, axis=1) if count > 1 else parts[0]


def weight_rows(ref, rows, tiles, first, count):
    shards = pl.ds(first // rows, count // rows)
    parts = [ref[shards, tile * rows : (tile + 1) * rows, :].reshape(count, 128) for tile in range(tiles)]
    return jnp.concatenate(parts, axis=1)


def norm_parts(values):
    center = values - jnp.mean(values, axis=-1, keepdims=True)
    scale = lax.rsqrt(jnp.mean(center * center, axis=-1, keepdims=True) + EPS)
    return center * scale, scale


def norm_back(hat, scale, pulled):
    down = jnp.mean(pulled, axis=-1, keepdims=True)
    along = jnp.mean(pulled * hat, axis=-1, keepdims=True)
    return scale * (pulled - down - hat * along)


def pack_kernel(qkv1, out1, merge, qkv2, out2, up, packed):
    for name, ref in (("qkv1", qkv1), ("out1", out1), ("merge", merge), ("qkv2", qkv2), ("out2", out2), ("up", up)):
        first, rows, tiles = PACK[name]
        for tile in range(tiles):
            packed[first + tile * rows : first + (tile + 1) * rows, :] = ref[:, tile * 128 : (tile + 1) * 128]


def ahead(own, lon, lat, diag, row, column):
    rows, columns = own.shape[0], own.shape[1]
    if row < rows and column < columns:
        return own.at[row, column]
    if row < rows:
        return lon.at[row]
    if column < columns:
        return lat.at[column]
    return diag.at[0]


def behind(own, lon, lat, diag, row, column):
    if row and column:
        return own.at[row, column]
    if row:
        return lon.at[row]
    if column:
        return lat.at[column]
    return diag.at[0]


def put_quarters(own, lon, lat, diag, row, column, value, lanes=slice(None)):
    own[row, column, :, lanes] = value
    if column == 0 and row:
        lon[row, :, lanes] = value
    if row == 0 and column:
        lat[column, :, lanes] = value
    if row == 0 and column == 0:
        diag[0, :, lanes] = value


def put_next(own, lon, lat, diag, row, column, value, lanes=slice(None)):
    ahead(own, lon, lat, diag, row + 1, column + 1)[:, lanes] = value


def window_spots(rows, columns):
    for row in range(rows):
        for column in range(columns):
            yield row, column, row // 2 * (columns // 2) + column // 2, (row % 2 * 2 + column % 2) * 32


def enter_kernel(
    tokens, cot, quarter_of_raw, merge_of_raw, own, lon, lat, diag, own_c, lon_c, lat_c, diag_c, padded, send
):
    padded[...] = jnp.zeros_like(padded)
    padded[:, :, 0:24, :] = tokens[...]
    for half in range(2):
        rows = padded[:, half * 6 : half * 6 + 6].reshape(576, 512)
        moved = nn(quarter_of_raw[...], rows).astype(BF)
        for quarter in range(16):
            row, column = quarter // 4 * 2 + quarter % 4 // 2, 2 * half + quarter % 2
            put_quarters(own, lon, lat, diag, row, column, moved[quarter * 32 : quarter * 32 + 32])
    send(0)
    padded[:, :, 0:24, :] = cot[...]
    for half in range(2):
        rows = padded[:, half * 6 : half * 6 + 6].reshape(576, 512)
        moved = nn(merge_of_raw[...], rows).astype(BF)
        for band in range(4):
            put_quarters(own_c, lon_c, lat_c, diag_c, band, half, moved[band * 128 : band * 128 + 128])
    send(1)


def head_masks():
    lane = lax.broadcasted_iota(jnp.int32, (1, 128), 1) // 32
    return [lane == head for head in range(4)]


def window_bias(usable_ref, flag_ref, window, windows, per_band):
    me = lax.broadcasted_iota(jnp.int32, (128, 128), 0)
    key = lax.broadcasted_iota(jnp.int32, (128, 128), 1)
    usable = usable_ref[pl.ds(window, 1), 0, :]
    cut = (flag_ref[0, 0] * jnp.where(window >= windows - per_band, 1, 0)).astype(jnp.int32)
    apart = jnp.where((me // 64) == (key // 64), 0, 1) * cut
    allowed = ((usable > 0.0) | (me == key)) & (apart == 0)
    return jnp.where(allowed, 0.0, BLOCKED)


def attend(field, w_qkv, w_out, usable, flag, qkv, raised, inverse, heads_out, per_band, emit):
    windows, _, width = field.shape
    tiles = width // 128
    shard = width // LONS

    def project(step, carry):
        weight = weight_columns(w_qkv, shard, 2 * step, 2)
        mixed = nn(field[...].reshape(windows * 128, width), weight).astype(BF)
        qkv[2 * step] = mixed[:, :128].reshape(windows, 128, 128)
        qkv[2 * step + 1] = mixed[:, 128:].reshape(windows, 128, 128)
        return carry

    lax.fori_loop(0, 3 * tiles // 2, project, 0)
    masks = head_masks()
    zero = jnp.zeros((), BF)
    ones = jnp.ones((128, 128), BF)

    def window_step(window, carry):
        bias = window_bias(usable, flag, window, windows, per_band)
        bias = jnp.concatenate([bias] * 4, axis=0)

        def tile_step(tile, carry):
            query, keys, values = qkv[tile, window], qkv[tiles + tile, window], qkv[2 * tiles + tile, window]
            queries = jnp.concatenate([jnp.where(mask, query, zero) for mask in masks], axis=0)
            power = jnp.exp2(nt(queries, keys) * (SCALE * LOG2E) + bias).astype(BF)
            raised[window, tile] = power
            side = jnp.concatenate([power[128 * head : 128 * head + 128] for head in range(4)], axis=1)
            stacked = jnp.concatenate(
                [
                    jnp.concatenate([jnp.where(mask, values, zero), jnp.where(mask, ones, zero)], axis=1)
                    for mask in masks
                ],
                axis=0,
            )
            both = nn(side, stacked)
            share = 1.0 / both[:, 128:]
            inverse[window, tile] = share
            heads_out[tile, window] = (both[:, :128] * share).astype(BF)
            return carry

        return lax.fori_loop(0, tiles, tile_step, carry)

    lax.fori_loop(0, windows, window_step, 0)
    heads = jnp.concatenate([heads_out[tile].reshape(windows * 128, 128) for tile in range(tiles)], axis=1)
    for step in range(tiles // 2):
        emit(slice(step * 256, step * 256 + 256), nn(heads, weight_columns(w_out, shard, 2 * step, 2)))


def attend_back(field, w_qkv, w_out, qkv, raised, inverse, heads_out, pulled, emit):
    windows, _, width = field.shape
    tiles = width // 128
    shard = width // LONS
    for step in range(tiles // 2):
        part = nt(field[...].reshape(windows * 128, width), weight_rows(w_out, shard, tiles, 256 * step, 256))
        part = part.astype(BF)
        pulled[2 * step] = part[:, :128].reshape(windows, 128, 128)
        pulled[2 * step + 1] = part[:, 128:].reshape(windows, 128, 128)
    masks = head_masks()
    zero = jnp.zeros((), BF)
    ones = jnp.ones((128, 128), BF)

    def stack(values):
        return jnp.concatenate([jnp.where(mask, values, zero) for mask in masks], axis=0)

    def tile_step(index, carry):
        window, tile = index // tiles, index % tiles
        query, keys, values = qkv[tile, window], qkv[tiles + tile, window], qkv[2 * tiles + tile, window]
        power = raised[window, tile]
        scaled = pulled[tile, window].astype(F32) * inverse[window, tile]
        taken = (scaled * heads_out[tile, window].astype(F32)).astype(BF)
        scaled_rows = stack(scaled.astype(BF))
        left = jnp.concatenate([scaled_rows, stack(-taken)], axis=1)
        slope = nt(left, jnp.concatenate([values, ones], axis=1))
        slope = (power.astype(F32) * slope).astype(BF)
        side = jnp.concatenate([slope[128 * head : 128 * head + 128] for head in range(4)], axis=1)
        pulled[2 * tiles + tile, window] = tn(power, scaled_rows).astype(BF)
        pulled[tiles + tile, window] = (tn(slope, stack(query)) * SCALE).astype(BF)
        pulled[tile, window] = (nn(side, stack(keys)) * SCALE).astype(BF)
        return carry

    lax.fori_loop(0, windows * tiles, tile_step, 0)
    pulls = jnp.concatenate([pulled[tile].reshape(windows * 128, 128) for tile in range(3 * tiles)], axis=1)
    for step in range(tiles // 2):
        emit(slice(step * 256, step * 256 + 256), nt(pulls, weight_rows(w_qkv, shard, 3 * tiles, 256 * step, 256)))


def first_kernel(
    own, lon, lat, diag, gain, w_qkv, w_out, usable, flag,
    own_o, lon_o, lat_o, diag_o, field, qkv, raised, inverse, heads_out, normed, send,
):
    for row, column, window, at in window_spots(8, 4):
        field[window, at : at + 32, :] = ahead(own, lon, lat, diag, row + 1, column + 1)[...]
    for window in range(8):
        hat, _ = norm_parts(field[window].astype(F32))
        normed[window] = (hat * gain[...]).astype(BF)

    def emit(lanes, result):
        result = result.astype(BF).astype(F32)
        for row, column, window, at in window_spots(8, 4):
            start = window * 128 + at
            stream = field[window, at : at + 32, lanes].astype(F32) + result[start : start + 32]
            put_quarters(own_o, lon_o, lat_o, diag_o, row, column, stream.astype(BF), lanes)

    attend(normed, w_qkv, w_out, usable, flag, qkv, raised, inverse, heads_out, 2, emit)
    send(0)


def first_back_kernel(
    own, lon, lat, diag, tokens, gain, w_qkv, w_out, qkv, raised, inverse, heads_out,
    own_o, lon_o, lat_o, diag_o, field, pulled, came, send,
):
    for row, column, window, at in window_spots(8, 4):
        field[window, at : at + 32, :] = behind(own, lon, lat, diag, row, column)[...]

    def emit(lanes, result):
        came[:, :, lanes] = result.reshape(8, 128, 256)

    attend_back(field, w_qkv, w_out, qkv, raised, inverse, heads_out, pulled, emit)
    for window in range(8):
        hat, scale = norm_parts(tokens[window].astype(F32))
        grad = norm_back(hat, scale, came[window] * gain[...])
        came[window] = field[window].astype(F32) + grad
    for row, column, window, at in window_spots(8, 4):
        value = came[window, at : at + 32, :].astype(BF)
        put_next(own_o, lon_o, lat_o, diag_o, row, column, value)
    send(0)


def members(block):
    return jnp.concatenate([block[32 * m : 32 * m + 32] for m in range(4)], axis=1)


def middle_kernel(
    own, lon, lat, diag, own_c, lon_c, lat_c, diag_c, w_merge, w_qkv, w_out, w_up,
    gain_merge, gain2, gain_up, usable, flag, merge_of_quarter, quarter_of_merge,
    own_o, lon_o, lat_o, diag_o, own_r, lon_r, lat_r, diag_r,
    stream, cot, wide, coarse, field, upper, spread, qkv, raised, inverse, heads_out, pulled, total, send,
):
    cells = [(cell, cell // 2, cell % 2) for cell in range(8)]
    for cell, row, column in cells:
        parts = [
            ahead(own, lon, lat, diag, 2 * row + q // 2 + 1, 2 * column + q % 2 + 1)[...] for q in range(4)
        ]
        block = nn(merge_of_quarter[...], jnp.concatenate(parts, axis=0))
        stream[cell] = block.astype(BF)
        cot[cell] = ahead(own_c, lon_c, lat_c, diag_c, row + 1, column + 1)[...]
        hat, _ = norm_parts(members(block))
        wide[32 * cell : 32 * cell + 32, :] = (hat * gain_merge[...]).astype(BF)
    for step in range(4):
        total[:, 256 * step : 256 * step + 256] = nn(wide[...], weight_columns(w_merge, 64, 2 * step, 2))
    values = total[...].astype(BF)
    coarse[...] = values
    hat, _ = norm_parts(values.astype(F32))
    field[...] = (hat * gain2[...]).astype(BF).reshape(2, 128, 1024)

    def add_coarse(lanes, result):
        result = result.astype(BF).astype(F32)
        upper[:, lanes] = (coarse[:, lanes].astype(F32) + result).astype(BF)

    attend(field, w_qkv, w_out, usable, flag, qkv, raised, inverse, heads_out, 1, add_coarse)
    for step in range(8):
        spread[:, 256 * step : 256 * step + 256] = nn(upper[...], weight_columns(w_up, 32, 2 * step, 2))
    for member in range(4):
        lanes = slice(512 * member, 512 * member + 512)
        hat, scale = norm_parts(spread[:, lanes])
        at = slice(32 * member, 32 * member + 32)
        skip = stream[:, at, :].reshape(256, 512).astype(F32)
        result = (skip + hat * gain_up[...]).astype(BF)
        for cell, row, column in cells:
            ahead(own_r, lon_r, lat_r, diag_r, row + 1, column + 1)[at, :] = result[32 * cell : 32 * cell + 32]
        pull = cot[:, at, :].reshape(256, 512).astype(F32) * gain_up[...]
        wide[:, lanes] = norm_back(hat, scale, pull).astype(BF)
    send(1)
    for step in range(4):
        lanes = slice(256 * step, 256 * step + 256)
        part = nt(wide[...], weight_rows(w_up, 32, 16, 256 * step, 256)).astype(BF)
        upper[:, lanes] = part
        field[:, :, lanes] = part.reshape(2, 128, 256)

    def keep(lanes, result):
        total[:, lanes] = result.astype(BF).astype(F32) * gain2[:, lanes]

    attend_back(field, w_qkv, w_out, qkv, raised, inverse, heads_out, pulled, keep)
    hat, scale = norm_parts(coarse[...].astype(F32))
    down = (upper[...].astype(F32) + norm_back(hat, scale, total[...])).astype(BF)
    for step in range(8):
        lanes = slice(256 * step, 256 * step + 256)
        wide[:, lanes] = nt(down, weight_rows(w_merge, 64, 8, 256 * step, 256)).astype(BF)
    for cell, row, column in cells:
        hat, scale = norm_parts(members(stream[cell].astype(F32)))
        grad = norm_back(hat, scale, wide[32 * cell : 32 * cell + 32, :].astype(F32) * gain_merge[...])
        grad = jnp.concatenate([grad[:, 512 * m : 512 * m + 512] for m in range(4)], axis=0)
        grad = (grad + cot[cell].astype(F32)).astype(BF)
        quarters = nn(quarter_of_merge[...], grad).astype(BF)
        for q in range(4):
            value = quarters[32 * q : 32 * q + 32]
            put_next(own_o, lon_o, lat_o, diag_o, 2 * row + q // 2, 2 * column + q % 2, value)
    send(0)


def leave_kernel(
    own, lon, lat, diag, own_r, lon_r, lat_r, diag_r, raw_of_quarter, raw_of_merge, grad, out,
):
    for half in range(2):
        parts = []
        for quarter in range(16):
            row, column = quarter // 4 * 2 + quarter % 4 // 2, 2 * half + quarter % 2
            parts.append(behind(own, lon, lat, diag, row, column)[...])
        moved = nn(raw_of_quarter[...], jnp.concatenate(parts, axis=0)).astype(BF).reshape(3, 6, 32, 512)
        grad[:, half * 6 : half * 6 + 6] = moved[:, :, 0:24, :]
        parts = [behind(own_r, lon_r, lat_r, diag_r, band, half)[...] for band in range(4)]
        moved = nn(raw_of_merge[...], jnp.concatenate(parts, axis=0)).astype(BF).reshape(3, 6, 32, 512)
        out[:, half * 6 : half * 6 + 6] = moved[:, :, 0:24, :]


WHOLE = pl.BlockSpec(memory_space=pltpu.VMEM)


def part_of(name):
    first, rows, tiles = PACK[name]
    size = rows * tiles
    return pl.BlockSpec((LONS, size, 128), lambda i: (0, first // size, 0), pipeline_mode=pl.Buffered(1))


def neighbours(step):
    lons, lats = lax.axis_size("lon"), lax.axis_size("lat")
    lon = lax.rem(lax.axis_index("lon") + (lons + step), lons)
    lat = lax.rem(lax.axis_index("lat") + (lats + step), lats)
    here = (lax.axis_index("lon"), lax.axis_index("lat"))
    return (lon, here[1]), (here[0], lat), (lon, lat)


def exchanging(body, ins, outs, moves, step):
    def kernel(*refs):
        operands, results, scratch = refs[:ins], list(refs[ins : ins + outs]), refs[ins + outs :]
        count = 3 * len(moves)
        pieces, send_sems, recv_sems = scratch[-count - 2 : -2], scratch[-2], scratch[-1]
        barrier = pltpu.get_barrier_semaphore()
        for device in neighbours(-step):
            pl.semaphore_signal(barrier, inc=1, device_id=device, device_id_type=pl.DeviceIdType.MESH)
        groups = []
        for group, at in enumerate(moves):
            copies = []
            for index, device in enumerate(neighbours(step)):
                source, target = pieces[3 * group + index], results[at + index]
                results[at + index] = source
                if index < 2:
                    used = pl.ds(1, source.shape[0] - 1)
                    source, target = source.at[used], target.at[used]
                copies.append(
                    pltpu.make_async_remote_copy(
                        src_ref=source,
                        dst_ref=target,
                        send_sem=send_sems.at[3 * group + index],
                        recv_sem=recv_sems.at[3 * group + index],
                        device_id=device,
                        device_id_type=pl.DeviceIdType.MESH,
                    )
                )
            groups.append(copies)
        greeted = []

        def send(group):
            if not greeted:
                pl.semaphore_wait(barrier, 3)
                greeted.append(True)
            for copy in groups[group]:
                copy.start()

        body(*operands, *results, *scratch[: -count - 2], send)
        for copies in groups:
            for copy in copies:
                copy.wait()

    return kernel


def call(body, outs, scratch, operands, packed=None, scalars=(), moves=(), step=0, number=0, name=None):
    specs, arrays = [], []
    for index, operand in enumerate(operands):
        if isinstance(operand, str):
            specs.append(part_of(operand))
            arrays.append(packed)
        elif index in scalars:
            specs.append(pl.BlockSpec(memory_space=pltpu.SMEM))
            arrays.append(operand)
        else:
            specs.append(WHOLE)
            arrays.append(operand)
    out_specs = [WHOLE] * len(outs)
    scratch = [pltpu.VMEM(shape, kind) for shape, kind in scratch]
    params = {}
    if moves:
        for at in moves:
            out_specs[at : at + 3] = [pl.BlockSpec(memory_space=pl.ANY)] * 3
            scratch += [pltpu.VMEM(shape, kind) for shape, kind in outs[at : at + 3]]
        scratch += [pltpu.SemaphoreType.DMA((3 * len(moves),))] * 2
        body = exchanging(body, len(operands), len(outs), moves, step)
        params = dict(collective_id=number, has_side_effects=True)
    return pl.pallas_call(
        body,
        grid=(1,),
        out_shape=[jax.ShapeDtypeStruct(shape, kind) for shape, kind in outs],
        in_specs=specs,
        out_specs=out_specs,
        scratch_shapes=scratch,
        compiler_params=pltpu.CompilerParams(vmem_limit_bytes=56 * MIB, **params),
        cost_estimate=pl.CostEstimate(flops=10**9, bytes_accessed=4 * MIB, transcendentals=0),
        name=name,
    )(*arrays)


def field_outs(rows, columns, tokens):
    return [
        ((rows, columns, tokens, 512), BF),
        ((rows, tokens, 512), BF),
        ((columns, tokens, 512), BF),
        ((1, tokens, 512), BF),
    ]


def kept(windows, tiles):
    return [
        ((3 * tiles, windows, 128, 128), BF),
        ((windows, tiles, 512, 128), BF),
        ((windows, tiles, 128, 128), F32),
        ((tiles, windows, 128, 128), BF),
    ]


def turned(field):
    return field.transpose(0, 2, 1, 3)


def usable_tokens(grid):
    rows, columns = grid.shape
    cells = grid.reshape(rows // 3, 3, columns // 3, 3).transpose(0, 2, 1, 3).reshape(rows // 3, columns // 3, 9)
    cells = jnp.pad(jnp.concatenate([cells] * 3, axis=2), ((0, 0), (0, 0), (0, 5)))
    cells = cells.reshape(rows // 6, 2, columns // 6, 2, 32).transpose(0, 2, 1, 3, 4)
    return cells.reshape(rows // 6 * (columns // 6), 1, 128).astype(F32)


def shards(
    tokens, valid, w_qkv1, w_out1, w_merge, w_qkv2, w_out2, w_up, gain1, gain_merge, gain2, gain_up, out_cot,
):
    (share,) = call(
        pack_kernel, [((PACK_ROWS, 128), BF)], [], [w_qkv1, w_out1, w_merge, w_qkv2, w_out2, w_up], name="pack"
    )
    packed = lax.all_gather(share, "lon", axis=0, tiled=False)
    merge_of_raw, quarter_of_raw, quarter_of_merge = (jnp.asarray(m, BF) for m in permutations())
    raw_of_merge, raw_of_quarter, merge_of_quarter = (
        jnp.asarray(np.ascontiguousarray(m.T), BF) for m in permutations()
    )
    gain1, gain_merge, gain2, gain_up = (g.reshape(1, -1) for g in (gain1, gain_merge, gain2, gain_up))

    lat_at, lon_at = lax.axis_index("lat"), lax.axis_index("lon")
    wide = jnp.concatenate([valid, valid[:6]], axis=0)
    wide = jnp.concatenate([wide, wide[:, :6]], axis=1)
    near = lax.dynamic_slice(wide, (lat_at * 24, lon_at * 12), (30, 18))
    usable1 = usable_tokens(near[3:27, 3:15])
    usable2 = usable_tokens(jnp.max(near[6:30, 6:18].reshape(12, 2, 6, 2), axis=(1, 3)))
    flag = (lat_at == lax.axis_size("lat") - 1).astype(jnp.int32).reshape(1, 1)

    fine, whole = field_outs(8, 4, 32), field_outs(4, 2, 128)
    came = call(
        enter_kernel,
        [*fine, *whole],
        [((3, 12, 32, 512), BF)],
        [turned(tokens), turned(out_cot), quarter_of_raw, merge_of_raw],
        moves=(1, 5),
        step=-1,
        number=0,
        name="enter",
    )
    cot = came[4:]
    result = call(
        first_kernel,
        [*fine, ((8, 128, 512), BF), *kept(8, 4)],
        [((8, 128, 512), BF)],
        [*came[:4], gain1, "qkv1", "out1", usable1, flag],
        packed=packed,
        scalars=(8,),
        moves=(1,),
        step=-1,
        number=1,
        name="first",
    )
    stream, windows, saved = result[:4], result[4], result[5:]
    result = call(
        middle_kernel,
        [*fine, *whole],
        [
            ((8, 128, 512), BF),
            ((8, 128, 512), BF),
            ((256, 2048), BF),
            ((256, 1024), BF),
            ((2, 128, 1024), BF),
            ((256, 1024), BF),
            ((256, 2048), F32),
            *kept(2, 8),
            ((24, 2, 128, 128), BF),
            ((256, 1024), F32),
        ],
        [
            *stream, *cot, "merge", "qkv2", "out2", "up",
            gain_merge, gain2, gain_up, usable2, flag, merge_of_quarter, quarter_of_merge,
        ],
        packed=packed,
        scalars=(16,),
        moves=(1, 5),
        step=1,
        number=2,
        name="middle",
    )
    stream_grad, output = result[:4], result[4:]
    grad = call(
        first_back_kernel,
        fine,
        [((8, 128, 512), BF), ((12, 8, 128, 128), BF), ((8, 128, 512), F32)],
        [*stream_grad, windows, gain1, "qkv1", "out1", *saved],
        packed=packed,
        moves=(1,),
        step=1,
        number=3,
        name="first_back",
    )
    grad_tokens, output = call(
        leave_kernel,
        [((3, 12, 24, 512), BF)] * 2,
        [],
        [*grad, *output, raw_of_quarter, raw_of_merge],
        name="leave",
    )
    return turned(output), turned(grad_tokens)


def solution(mesh):
    placed = (P(None, "lat", "lon", None), P(), *[P("lon", None)] * 6, *[P()] * 4, P(None, "lat", "lon", None))
    return jax.shard_map(
        shards,
        mesh=mesh,
        in_specs=placed,
        out_specs=(P(None, "lat", "lon", None), P(None, "lat", "lon", None)),
        check_vma=False,
    )
```

profile of v0, /device:TPU:0, one launch (start us, length us, event | category | flops | bytes accessed | tf_op | source)
XLA Modules:
  0.0 253.2 jit_solution(9503354592503152263)
XLA Ops:
  7.2 0.0 copy-start
  7.2 0.0 all-gather.3.cloned.1.call-start
  7.2 2.1 pack.1
  9.3 0.0 all-gather.3.cloned.1.call-update
  9.3 0.0 copy-done
  9.4 0.1 fusion.1
  9.5 0.1 fusion.2
  9.6 0.1 copy.36
  9.6 0.1 copy.30
  9.7 0.1 reshape.66
  9.8 0.1 copy.31
  10.0 0.1 copy.32
  10.1 0.1 pad_add_fusion.1
  10.2 0.7 convert_element_type.18.refs_7_
  10.9 0.1 reshape.73
  11.0 0.2 reduce_max.9
  11.2 0.1 reshape.74
  11.2 0.1 copy.37
  11.4 0.1 copy.38
  11.5 0.1 pad_add_fusion.2
  11.6 0.6 convert_element_type.20.refs_15_
  12.2 26.9 %enter.1 = (bf16[8,4,32,512]{3,2,1,0:T(8,128)(2,1)}, bf16[8,32,512]{2,1,0:T(8,128)(2,1)}, bf16[4,32,512]{2,1,0:T(8,128)(2,1)}, bf16[1,32,512]{2,1,0:T(8,128)(2,1...) custom-call(bf16[3,12,24,512]{3,2,1,0:T(8,128)(2,1)} %bitcast.41, ...), custom_call_target="tpu_custom_call" | custom-call | flops 1000000000 | bytes 4194304 | tf_op jit(solution)/shard_map/enter/pallas_call | solution.py:471
  39.1 90.1 %all-gather.3.cloned.1.call-done = bf16[73728,128]{1,0:T(8,128)(2,1)} async-done(((bf16[2304,128]{1,0:T(8,128)(2,1)}), bf16[73728,128]{1,0:T(8,128)(2,1)}) %all-gather.3.cloned.1.call-update) | async-done | bytes 18874384 | tf_op jit(solution)/shard_map/all_gather | solution.py:520
  129.2 27.1 %first.1 = (bf16[8,4,32,512]{3,2,1,0:T(8,128)(2,1)}, bf16[8,32,512]{2,1,0:T(8,128)(2,1)}, bf16[4,32,512]{2,1,0:T(8,128)(2,1)}, bf16[1,32,512]{2,1,0:T(8,128)(2,1...) custom-call(bf16[8,4,32,512]{3,2,1,0:T(8,128)(2,1)} %get-tuple-eleme, ...), custom_call_target="tpu_custom_call" | custom-call | flops 1000000000 | bytes 4194304 | tf_op jit(solution)/shard_map/first/pallas_call | solution.py:471
  156.3 51.8 %middle.1 = (bf16[8,4,32,512]{3,2,1,0:T(8,128)(2,1)}, bf16[8,32,512]{2,1,0:T(8,128)(2,1)}, bf16[4,32,512]{2,1,0:T(8,128)(2,1)}, bf16[1,32,512]{2,1,0:T(8,128)(2,...) custom-call(bf16[8,4,32,512]{3,2,1,0:T(8,128)(2,1)} %get-tuple-eleme, ...), custom_call_target="tpu_custom_call" | custom-call | flops 1000000000 | bytes 4194304 | tf_op jit(solution)/shard_map/middle/pallas_call | solution.py:471
  208.2 33.6 %first_back.1 = (bf16[8,4,32,512]{3,2,1,0:T(8,128)(2,1)}, bf16[8,32,512]{2,1,0:T(8,128)(2,1)}, bf16[4,32,512]{2,1,0:T(8,128)(2,1)}, bf16[1,32,512]{2,1,0:T(8,128)(2,1)}) custom-call(bf16[8,4,32,512]{3,2,1,0:T(8,128)(2,1)} %get-tuple-element.45.refs_0_, bf16[8,32,512]{2,1,0:T(8,128)(2,1)} %get-tuple-element.46.refs_1_, ...), custom_call_target="tpu_custom_call" | custom-call | flops 1000000000 | bytes 4194304 | tf_op jit(solution)/shard_map/first_back/pallas_call | solution.py:471
  241.8 4.6 %leave.1 = (bf16[3,12,24,512]{3,2,1,0:T(8,128)(2,1)}, bf16[3,12,24,512]{3,2,1,0:T(8,128)(2,1)}) custom-call(bf16[8,4,32,512]{3,2,1,0:T(8,128)(2,1)} %get-tuple-element.54.own, bf16[8,32,512]{2,1,0:T(8,128)(2,1)} %get-tuple-element.55.lon, bf16[4,32,512]{2,1,0:T(8,128)(2,1)} %get-tuple-element.56.lat, bf16[1,32,512]{2,1,0:T(8,128)(2,1)} %get-tuple-element.57.diag, ...), custom_call_target="tpu_custom_call" | custom-call | flops 1000000000 | bytes 4194304 | tf_op jit(solution)/shard_map/leave/pallas_call | solution.py:471
  (6 shorter events, 0.1 us)
Async XLA Ops:
  7.2 2.2 copy-start
  7.2 122.0 %all-gather.3.cloned.1.call-start = ((), (), s32[]{:S(2)}) async-start(), calls=%async_computation | async-start | bytes 19464192 | tf_op jit(solution)/shard_map/all_gather | solution.py:520
Sparse Core Ops, SparseCore 0:
  10.4 118.6 all-gather.2
where the time goes:
time: 255 us; the launch traced here: 253 us
  Pallas kernels  146 us (57%)
  waiting for transfers between devices  90.1 us (35%)
  between operations  14.2 us (6%)
    pallas_call x6, Pallas kernels, call(): pl.pallas_call(body, grid=(1,), out_shape=[jax.ShapeDtypeStruct(shape, ki...  146 us
    all_gather x1, waiting for transfers between devices, shards(): packed = lax.all_gather(share, 'lon', axis=0, tiled=False)  90.1 us
  transfers between devices with their start and end apart: 1, of which 1 were waited for; matrix products, arithmetic and copies ran while one was open for 1% of the time, Pallas kernels for 11%

commit v1 on v0

--- a/solution.py
+++ b/solution.py
@@ -15,14 +15,16 @@
 MIB = 1024 * 1024
 
 PACK = {
-    "qkv2": (0, 32, 24),
-    "out2": (768, 32, 8),
-    "merge": (1024, 64, 8),
-    "up": (1536, 32, 16),
-    "out1": (2048, 16, 4),
-    "qkv1": (2112, 16, 12),
+    "qkv1": (0, 0, 16, 12),
+    "out1": (0, 192, 16, 4),
+    "qkv2": (1, 0, 32, 24),
+    "out2": (1, 768, 32, 8),
+    "merge": (1, 1024, 64, 8),
+    "up": (1, 1536, 32, 16),
 }
-PACK_ROWS = 2304
+SHARE_ROWS = (256, 2048)
+ROUNDS = ("z", "p1", "p2", "q1", "q2", "r1", "r2", "r3")
+COPIES = 38
 SCALE = 32.0**-0.5
 LOG2E = 1.4426950408889634
 BLOCKED = -1e30
@@ -85,11 +87,134 @@
     return scale * (pulled - down - hat * along)
 
 
-def pack_kernel(qkv1, out1, merge, qkv2, out2, up, packed):
-    for name, ref in (("qkv1", qkv1), ("out1", out1), ("merge", merge), ("qkv2", qkv2), ("out2", out2), ("up", up)):
-        first, rows, tiles = PACK[name]
+def pack(shares, **weights):
+    for name, ref in weights.items():
+        share, first, rows, tiles = PACK[name]
         for tile in range(tiles):
-            packed[first + tile * rows : first + (tile + 1) * rows, :] = ref[:, tile * 128 : (tile + 1) * 128]
+            at = slice(first + tile * rows, first + (tile + 1) * rows)
+            shares[share][at, :] = ref[:, tile * 128 : (tile + 1) * 128]
+
+
+def place():
+    lon, lat = lax.axis_index("lon"), lax.axis_index("lat")
+    return lat % 2 * 2 + lon // 2 % 2, lat // 2, lon // 4, lon % 2
+
+
+def device_at(x, y, z, core):
+    return z * 4 + x % 2 * 2 + core, y * 2 + x // 2
+
+
+def gather_peers(rounds):
+    x, y, z, core = place()
+    peers = [device_at(x, y, (z + step) % 8, core) for step in range(1, 8)] if "z" in rounds else []
+    peers += [device_at((x + step) % 4, y, z, core) for step in (1, 3)]
+    peers += [device_at(x, (y + step) % 4, z, core) for step in (1, 3)]
+    return peers + [device_at(x, y, z, 1 - core)]
+
+
+def gather_rounds(share, whole, send_sems, recv_sems):
+    x, y, z, core = place()
+    part = whole.shape[3] // 16
+    half = 8 * part
+    plus_x, minus_x, plus_y, minus_y = (x + 1) % 4, (x + 3) % 4, (y + 1) % 4, (y + 3) % 4
+    low, high = pl.ds(0, 4), pl.ds(4, 4)
+    every = pl.ds(0, 8)
+
+    def rows(start, count):
+        return pl.ds(pl.multiple_of(start, 16), count)
+
+    def one(x, y):
+        return rows((y * 2 + x // 2) * part, part)
+
+    def two(x, y):
+        return rows(half + (x // 2 * 4 + y) * part, part)
+
+    def slab(which, zs, x, y):
+        return whole.at[zs, x % 2, core, which(x, y)]
+
+    def across(zs, y):
+        return whole.at[zs, :, core, rows(y * 2 * part, 2 * part)]
+
+    def along(zs, x):
+        return whole.at[zs, x % 2, core, rows(half + x // 2 * 4 * part, 4 * part)]
+
+    to = {
+        "+x": device_at(plus_x, y, z, core),
+        "-x": device_at(minus_x, y, z, core),
+        "+y": device_at(x, plus_y, z, core),
+        "-y": device_at(x, minus_y, z, core),
+        "twin": device_at(x, y, z, 1 - core),
+    }
+    far_x, far_y = (x + 2) % 4, (y + 2) % 4
+    plan = {
+        "p1": [
+            (slab(one, every, x, y), "+x"),
+            (slab(one, every, x, y), "-x"),
+            (slab(two, every, x, y), "+y"),
+            (slab(two, every, x, y), "-y"),
+        ],
+        "p2": [
+            (slab(one, low, minus_x, y), "+x"),
+            (slab(one, high, plus_x, y), "-x"),
+            (slab(two, low, x, minus_y), "+y"),
+            (slab(two, high, x, plus_y), "-y"),
+        ],
+        "q1": [(across(every, y), "+y"), (across(every, y), "-y"), (along(every, x), "+x"), (along(every, x), "-x")],
+        "q2": [
+            (across(low, minus_y), "+y"),
+            (across(high, plus_y), "-y"),
+            (along(low, minus_x), "+x"),
+            (along(high, plus_x), "-x"),
+        ],
+        "r1": [(across(every, y), "twin"), (along(every, x), "twin")],
+        "r2": [
+            (across(every, minus_y), "twin"),
+            (across(every, plus_y), "twin"),
+            (along(every, minus_x), "twin"),
+            (along(every, plus_x), "twin"),
+        ],
+        "r3": [(across(every, far_y), "twin"), (along(every, far_x), "twin")],
+    }
+    made, count = {"z": [], "own": []}, 0
+
+    def remote(source, target, device):
+        nonlocal count
+        count += 1
+        return pltpu.make_async_remote_copy(
+            src_ref=source,
+            dst_ref=target,
+            send_sem=send_sems.at[count - 1],
+            recv_sem=recv_sems.at[count - 1],
+            device_id=device,
+            device_id_type=pl.DeviceIdType.MESH,
+        )
+
+    for which in (one, two):
+        here = whole.at[z, x % 2, core, which(x, y)]
+        for step in range(1, 8):
+            source = here if share is None else share.at[which(x, y)]
+            made["z"].append(remote(source, here, device_at(x, y, (z + step) % 8, core)))
+        if share is not None:
+            own = pltpu.make_async_copy(share.at[which(x, y)], here, send_sems.at[COPIES + len(made["own"])])
+            made["own"].append(own)
+    for name, copies in plan.items():
+        made[name] = [remote(piece, piece, to[device]) for piece, device in copies]
+    return made
+
+
+def start(copies):
+    for copy in copies:
+        copy.start()
+
+
+def arrive(copies):
+    for copy in copies:
+        copy.wait_recv()
+
+
+def left(copies):
+    for copy in copies:
+        copy.wait_send()
 
 
 def ahead(own, lon, lat, diag, row, column):
@@ -134,8 +259,16 @@
 
 
 def enter_kernel(
-    tokens, cot, quarter_of_raw, merge_of_raw, own, lon, lat, diag, own_c, lon_c, lat_c, diag_c, padded, send
+    tokens, cot, quarter_of_raw, merge_of_raw, qkv1, out1, merge, qkv2, out2, up,
+    own, lon, lat, diag, own_c, lon_c, lat_c, diag_c, whole1, whole2,
+    padded, share1, share2, sends1, recvs1, sends2, recvs2, greet, send,
 ):
+    shares = (share1, share2)
+    pack(shares, qkv1=qkv1, out1=out1)
+    first = gather_rounds(share1, whole1, sends1, recvs1)
+    rest = gather_rounds(share2, whole2, sends2, recvs2)
+    greet()
+    start(first["z"] + first["own"])
     padded[...] = jnp.zeros_like(padded)
     padded[:, :, 0:24, :] = tokens[...]
     for half in range(2):
@@ -145,13 +278,38 @@
             row, column = quarter // 4 * 2 + quarter % 4 // 2, 2 * half + quarter % 2
             put_quarters(own, lon, lat, diag, row, column, moved[quarter * 32 : quarter * 32 + 32])
     send(0)
+    arrive(first["z"])
+    for copy in first["own"]:
+        copy.wait()
+    start(first["p1"])
+    pack(shares, merge=merge, qkv2=qkv2, out2=out2, up=up)
+    start(rest["z"] + rest["own"])
+    arrive(first["p1"])
+    start(first["p2"])
     padded[:, :, 0:24, :] = cot[...]
     for half in range(2):
         rows = padded[:, half * 6 : half * 6 + 6].reshape(576, 512)
         moved = nn(merge_of_raw[...], rows).astype(BF)
         for band in range(4):
             put_quarters(own_c, lon_c, lat_c, diag_c, band, half, moved[band * 128 : band * 128 + 128])
+    arrive(first["p2"])
+    start(first["q1"] + first["r1"])
+    arrive(rest["z"])
+    for copy in rest["own"]:
+        copy.wait()
+    arrive(first["q1"])
+    start(first["q2"] + first["r2"])
+    start(rest["p1"])
     send(1)
+    arrive(first["q2"])
+    start(first["r3"])
+    arrive(rest["p1"])
+    start(rest["p2"])
+    arrive(first["r1"] + first["r2"] + first["r3"])
+    arrive(rest["p2"])
+    for name in ROUNDS:
+        left(first[name])
+    left(rest["z"] + rest["p1"] + rest["p2"])
 
 
 def head_masks():
@@ -256,9 +414,12 @@
 
 
 def first_kernel(
-    own, lon, lat, diag, gain, w_qkv, w_out, usable, flag,
-    own_o, lon_o, lat_o, diag_o, field, qkv, raised, inverse, heads_out, normed, send,
+    own, lon, lat, diag, gain, w_qkv, w_out, usable, flag, whole_in,
+    own_o, lon_o, lat_o, diag_o, field, qkv, raised, inverse, heads_out, whole, normed, sends, recvs, greet, send,
 ):
+    rest = gather_rounds(None, whole, sends, recvs)
+    greet()
+    start(rest["q1"] + rest["r1"])
     for row, column, window, at in window_spots(8, 4):
         field[window, at : at + 32, :] = ahead(own, lon, lat, diag, row + 1, column + 1)[...]
     for window in range(8):
@@ -274,11 +435,18 @@
 
     attend(normed, w_qkv, w_out, usable, flag, qkv, raised, inverse, heads_out, 2, emit)
     send(0)
+    arrive(rest["q1"])
+    start(rest["q2"] + rest["r2"])
+    arrive(rest["q2"])
+    start(rest["r3"])
+    arrive(rest["r1"] + rest["r2"] + rest["r3"])
+    for name in ROUNDS[3:]:
+        left(rest[name])
 
 
 def first_back_kernel(
     own, lon, lat, diag, tokens, gain, w_qkv, w_out, qkv, raised, inverse, heads_out,
-    own_o, lon_o, lat_o, diag_o, field, pulled, came, send,
+    own_o, lon_o, lat_o, diag_o, field, pulled, came, greet, send,
 ):
     for row, column, window, at in window_spots(8, 4):
         field[window, at : at + 32, :] = behind(own, lon, lat, diag, row, column)[...]
@@ -294,6 +462,7 @@
     for row, column, window, at in window_spots(8, 4):
         value = came[window, at : at + 32, :].astype(BF)
         put_next(own_o, lon_o, lat_o, diag_o, row, column, value)
+    greet()
     send(0)
 
 
@@ -305,7 +474,7 @@
     own, lon, lat, diag, own_c, lon_c, lat_c, diag_c, w_merge, w_qkv, w_out, w_up,
     gain_merge, gain2, gain_up, usable, flag, merge_of_quarter, quarter_of_merge,
     own_o, lon_o, lat_o, diag_o, own_r, lon_r, lat_r, diag_r,
-    stream, cot, wide, coarse, field, upper, spread, qkv, raised, inverse, heads_out, pulled, total, send,
+    stream, cot, wide, coarse, field, upper, spread, qkv, raised, inverse, heads_out, pulled, total, greet, send,
 ):
     cells = [(cell, cell // 2, cell % 2) for cell in range(8)]
     for cell, row, column in cells:
@@ -341,6 +510,7 @@
             ahead(own_r, lon_r, lat_r, diag_r, row + 1, column + 1)[at, :] = result[32 * cell : 32 * cell + 32]
         pull = cot[:, at, :].reshape(256, 512).astype(F32) * gain_up[...]
         wide[:, lanes] = norm_back(hat, scale, pull).astype(BF)
+    greet()
     send(1)
     for step in range(4):
         lanes = slice(256 * step, 256 * step + 256)
@@ -388,7 +558,7 @@
 
 
 def part_of(name):
-    first, rows, tiles = PACK[name]
+    _, first, rows, tiles = PACK[name]
     size = rows * tiles
     return pl.BlockSpec((LONS, size, 128), lambda i: (0, first // size, 0), pipeline_mode=pl.Buffered(1))
 
@@ -401,13 +571,14 @@
     return (lon, here[1]), (here[0], lat), (lon, lat)
 
 
-def exchanging(body, ins, outs, moves, step):
+def exchanging(body, ins, outs, moves, step, rounds):
     def kernel(*refs):
         operands, results, scratch = refs[:ins], list(refs[ins : ins + outs]), refs[ins + outs :]
         count = 3 * len(moves)
         pieces, send_sems, recv_sems = scratch[-count - 2 : -2], scratch[-2], scratch[-1]
         barrier = pltpu.get_barrier_semaphore()
-        for device in neighbours(-step):
+        others = gather_peers(rounds) if rounds else []
+        for device in [*neighbours(-step), *others]:
             pl.semaphore_signal(barrier, inc=1, device_id=device, device_id_type=pl.DeviceIdType.MESH)
         groups = []
         for group, at in enumerate(moves):
@@ -429,16 +600,13 @@
                     )
                 )
             groups.append(copies)
-        greeted = []
+        def greet():
+            pl.semaphore_wait(barrier, 3 + len(others))
 
         def send(group):
-            if not greeted:
-                pl.semaphore_wait(barrier, 3)
-                greeted.append(True)
-            for copy in groups[group]:
-                copy.start()
-
-        body(*operands, *results, *scratch[: -count - 2], send)
+            start(groups[group])
+
+        body(*operands, *results, *scratch[: -count - 2], greet, send)
         for copies in groups:
             for copy in copies:
                 copy.wait()
@@ -446,12 +614,12 @@
     return kernel
 
 
-def call(body, outs, scratch, operands, packed=None, scalars=(), moves=(), step=0, number=0, name=None):
+def call(body, outs, scratch, operands, packed=None, scalars=(), moves=(), step=0, number=0, rounds=(), wholes=(), name=None):
     specs, arrays = [], []
     for index, operand in enumerate(operands):
         if isinstance(operand, str):
             specs.append(part_of(operand))
-            arrays.append(packed)
+            arrays.append(packed[PACK[operand][0]])
         elif index in scalars:
             specs.append(pl.BlockSpec(memory_space=pltpu.SMEM))
             arrays.append(operand)
@@ -459,14 +627,19 @@
             specs.append(WHOLE)
             arrays.append(operand)
     out_specs = [WHOLE] * len(outs)
-    scratch = [pltpu.VMEM(shape, kind) for shape, kind in scratch]
-    params = {}
+    scratch = [pltpu.VMEM(*item) if isinstance(item, tuple) else item for item in scratch]
+    params, aliases = {}, {}
+    for at in wholes:
+        out_specs[at] = pl.BlockSpec(memory_space=pl.ANY)
+    if rounds and "z" not in rounds:
+        specs[-1] = pl.BlockSpec(memory_space=pl.ANY)
+        aliases = {len(specs) - 1: wholes[0]}
     if moves:
         for at in moves:
             out_specs[at : at + 3] = [pl.BlockSpec(memory_space=pl.ANY)] * 3
             scratch += [pltpu.VMEM(shape, kind) for shape, kind in outs[at : at + 3]]
         scratch += [pltpu.SemaphoreType.DMA((3 * len(moves),))] * 2
-        body = exchanging(body, len(operands), len(outs), moves, step)
+        body = exchanging(body, len(operands), len(outs), moves, step, rounds)
         params = dict(collective_id=number, has_side_effects=True)
     return pl.pallas_call(
         body,
@@ -475,6 +648,7 @@
         in_specs=specs,
         out_specs=out_specs,
         scratch_shapes=scratch,
+        input_output_aliases=aliases,
         compiler_params=pltpu.CompilerParams(vmem_limit_bytes=56 * MIB, **params),
         cost_estimate=pl.CostEstimate(flops=10**9, bytes_accessed=4 * MIB, transcendentals=0),
         name=name,
@@ -514,10 +688,6 @@
 def shards(
     tokens, valid, w_qkv1, w_out1, w_merge, w_qkv2, w_out2, w_up, gain1, gain_merge, gain2, gain_up, out_cot,
 ):
-    (share,) = call(
-        pack_kernel, [((PACK_ROWS, 128), BF)], [], [w_qkv1, w_out1, w_merge, w_qkv2, w_out2, w_up], name="pack"
-    )
-    packed = lax.all_gather(share, "lon", axis=0, tiled=False)
     merge_of_raw, quarter_of_raw, quarter_of_merge = (jnp.asarray(m, BF) for m in permutations())
     raw_of_merge, raw_of_quarter, merge_of_quarter = (
         jnp.asarray(np.ascontiguousarray(m.T), BF) for m in permutations()
@@ -535,28 +705,41 @@
     fine, whole = field_outs(8, 4, 32), field_outs(4, 2, 128)
     came = call(
         enter_kernel,
-        [*fine, *whole],
-        [((3, 12, 32, 512), BF)],
-        [turned(tokens), turned(out_cot), quarter_of_raw, merge_of_raw],
+        [*fine, *whole, *[((8, 2, 2, rows, 128), BF) for rows in SHARE_ROWS]],
+        [
+            ((3, 12, 32, 512), BF),
+            *[((rows, 128), BF) for rows in SHARE_ROWS],
+            *[pltpu.SemaphoreType.DMA((COPIES + 2,)), pltpu.SemaphoreType.DMA((COPIES,))] * 2,
+        ],
+        [
+            turned(tokens), turned(out_cot), quarter_of_raw, merge_of_raw,
+            w_qkv1, w_out1, w_merge, w_qkv2, w_out2, w_up,
+        ],
         moves=(1, 5),
         step=-1,
         number=0,
+        rounds=ROUNDS,
+        wholes=(8, 9),
         name="enter",
     )
-    cot = came[4:]
+    cot = came[4:8]
+    packed = [came[8].reshape(LONS, -1, 128)]
     result = call(
         first_kernel,
-        [*fine, ((8, 128, 512), BF), *kept(8, 4)],
-        [((8, 128, 512), BF)],
-        [*came[:4], gain1, "qkv1", "out1", usable1, flag],
+        [*fine, ((8, 128, 512), BF), *kept(8, 4), ((8, 2, 2, SHARE_ROWS[1], 128), BF)],
+        [((8, 128, 512), BF), pltpu.SemaphoreType.DMA((COPIES,)), pltpu.SemaphoreType.DMA((COPIES,))],
+        [*came[:4], gain1, "qkv1", "out1", usable1, flag, came[9]],
         packed=packed,
         scalars=(8,),
         moves=(1,),
         step=-1,
         number=1,
+        rounds=ROUNDS[3:],
+        wholes=(9,),
         name="first",
     )
-    stream, windows, saved = result[:4], result[4], result[5:]
+    stream, windows, saved = result[:4], result[4], result[5:9]
+    packed.append(result[9].reshape(LONS, -1, 128))
     result = call(
         middle_kernel,
         [*fine, *whole],

time: 255 us -> 200 us (0.78)
  waiting for transfers between devices: 90.1 us -> 0 us
  Pallas kernels: 146 us -> 191 us
  between operations: 14.2 us -> 0.72 us
    all_gather x1 -> x0, waiting for transfers between devices: 90.1 us -> none  [shards(): packed = lax.all_gather(share, 'lon', axis=0, tiled=False)]
    pallas_call x6 -> x5, Pallas kernels: 146 us -> 191 us  [call(): pl.pallas_call(body, grid=(1,), out_shape=[jax.ShapeDtypeStruct(shape, ki...]
  transfers between devices with their start and end apart: 1 -> 0, of which waited for: 1 -> 0; matrix products, arithmetic and copies ran while one was open for 1% -> 0% of each run, Pallas kernels for 11% -> 0%
where the time goes in v1:
time: 200 us; the launch traced here: 197 us
  Pallas kernels  191 us (96%)
  local copies, waits for them, and re-layouts  3.03 us (2%)
  other arithmetic  2.12 us (1%)
    pallas_call x5, Pallas kernels, call(): pl.pallas_call(body, grid=(1,), out_shape=[jax.ShapeDtypeStruct(shape, ki...  191 us

profile of v1, /device:TPU:0, one launch (start us, length us, event | category | flops | bytes accessed | tf_op | source)
XLA Modules:
  0.0 197.3 jit_solution(10439919652370048400)
XLA Ops:
  0.6 0.7 slice.12
  1.3 0.9 pad_add_fusion
  2.2 0.9 fusion.1
  3.1 0.1 fusion.2
  3.2 0.1 copy.37
  3.3 0.1 copy.31
  3.4 0.1 reshape.73
  3.5 0.1 copy.32
  3.6 0.1 copy.33
  3.7 0.1 pad_add_fusion.1
  3.8 0.7 convert_element_type.18.refs_7_
  4.5 0.1 reshape.81
  4.6 0.2 reduce_max.9
  4.8 0.1 reshape.82
  4.9 0.1 copy.38
  5.0 0.1 copy.39
  5.1 0.1 pad_add_fusion.2
  5.2 0.7 convert_element_type.20.refs_15_
  5.8 49.7 %enter.1 = (bf16[8,4,32,512]{3,2,1,0:T(8,128)(2,1)}, bf16[8,32,512]{2,1,0:T(8,128)(2,1)}, bf16[4,32,512]{2,1,0:T(8,128)(2,1)}, bf16[1,32,512]{2,1,0:T(8,128)(2,1...) custom-call(bf16[3,12,24,512]{3,2,1,0:T(8,128)(2,1)} %bitcast.42, ...), custom_call_target="tpu_custom_call" | custom-call | flops 1000000000 | bytes 4194304 | tf_op jit(solution)/shard_map/enter/pallas_call | solution.py:644
  55.5 56.1 %first.1 = (bf16[8,4,32,512]{3,2,1,0:T(8,128)(2,1)}, bf16[8,32,512]{2,1,0:T(8,128)(2,1)}, bf16[4,32,512]{2,1,0:T(8,128)(2,1)}, bf16[1,32,512]{2,1,0:T(8,128)(2,1...) custom-call(bf16[8,4,32,512]{3,2,1,0:T(8,128)(2,1)} %get-tuple-eleme, ...), custom_call_target="tpu_custom_call", output_to_operand_aliasing={{9}: (9, {})} | custom-call | flops 1000000000 | bytes 4194304 | tf_op jit(solution)/shard_map/first/pallas_call | solution.py:644
  111.7 47.3 %middle.1 = (bf16[8,4,32,512]{3,2,1,0:T(8,128)(2,1)}, bf16[8,32,512]{2,1,0:T(8,128)(2,1)}, bf16[4,32,512]{2,1,0:T(8,128)(2,1)}, bf16[1,32,512]{2,1,0:T(8,128)(2,...) custom-call(bf16[8,4,32,512]{3,2,1,0:T(8,128)(2,1)} %get-tuple-eleme, ...), custom_call_target="tpu_custom_call" | custom-call | flops 1000000000 | bytes 4194304 | tf_op jit(solution)/shard_map/middle/pallas_call | solution.py:644
  159.0 33.7 %first_back.1 = (bf16[8,4,32,512]{3,2,1,0:T(8,128)(2,1)}, bf16[8,32,512]{2,1,0:T(8,128)(2,1)}, bf16[4,32,512]{2,1,0:T(8,128)(2,1)}, bf16[1,32,512]{2,1,0:T(8,128)(2,1)}) custom-call(bf16[8,4,32,512]{3,2,1,0:T(8,128)(2,1)} %get-tuple-element.51.refs_0_, bf16[8,32,512]{2,1,0:T(8,128)(2,1)} %get-tuple-element.52.refs_1_, ...), custom_call_target="tpu_custom_call" | custom-call | flops 1000000000 | bytes 4194304 | tf_op jit(solution)/shard_map/first_back/pallas_call | solution.py:644
  192.7 4.6 %leave.1 = (bf16[3,12,24,512]{3,2,1,0:T(8,128)(2,1)}, bf16[3,12,24,512]{3,2,1,0:T(8,128)(2,1)}) custom-call(bf16[8,4,32,512]{3,2,1,0:T(8,128)(2,1)} %get-tuple-element.60.own, bf16[8,32,512]{2,1,0:T(8,128)(2,1)} %get-tuple-element.61.lon, bf16[4,32,512]{2,1,0:T(8,128)(2,1)} %get-tuple-element.62.lat, bf16[1,32,512]{2,1,0:T(8,128)(2,1)} %get-tuple-element.63.diag, ...), custom_call_target="tpu_custom_call" | custom-call | flops 1000000000 | bytes 4194304 | tf_op jit(solution)/shard_map/leave/pallas_call | solution.py:644
  (4 shorter events, 0.0 us)

commit v2 on v1

--- a/solution.py
+++ b/solution.py
@@ -348,11 +348,9 @@
         bias = window_bias(usable, flag, window, windows, per_band)
         bias = jnp.concatenate([bias] * 4, axis=0)
 
-        def tile_step(tile, carry):
-            query, keys, values = qkv[tile, window], qkv[tiles + tile, window], qkv[2 * tiles + tile, window]
+        def weigh(query, keys, values):
             queries = jnp.concatenate([jnp.where(mask, query, zero) for mask in masks], axis=0)
             power = jnp.exp2(nt(queries, keys) * (SCALE * LOG2E) + bias).astype(BF)
-            raised[window, tile] = power
             side = jnp.concatenate([power[128 * head : 128 * head + 128] for head in range(4)], axis=1)
             stacked = jnp.concatenate(
                 [
@@ -363,11 +361,19 @@
             )
             both = nn(side, stacked)
             share = 1.0 / both[:, 128:]
-            inverse[window, tile] = share
-            heads_out[tile, window] = (both[:, :128] * share).astype(BF)
+            return power, share, (both[:, :128] * share).astype(BF)
+
+        def tile_step(step, carry):
+            pair = (2 * step, 2 * step + 1)
+            loaded = [[qkv[part * tiles + tile, window] for part in range(3)] for tile in pair]
+            made = [weigh(*operands) for operands in loaded]
+            for tile, (power, share, out) in zip(pair, made):
+                raised[window, tile] = power
+                inverse[window, tile] = share
+                heads_out[tile, window] = out
             return carry
 
-        return lax.fori_loop(0, tiles, tile_step, carry)
+        return lax.fori_loop(0, tiles // 2, tile_step, carry)
 
     lax.fori_loop(0, windows, window_step, 0)
     heads = jnp.concatenate([heads_out[tile].reshape(windows * 128, 128) for tile in range(tiles)], axis=1)
@@ -391,23 +397,34 @@
     def stack(values):
         return jnp.concatenate([jnp.where(mask, values, zero) for mask in masks], axis=0)
 
-    def tile_step(index, carry):
-        window, tile = index // tiles, index % tiles
-        query, keys, values = qkv[tile, window], qkv[tiles + tile, window], qkv[2 * tiles + tile, window]
-        power = raised[window, tile]
-        scaled = pulled[tile, window].astype(F32) * inverse[window, tile]
-        taken = (scaled * heads_out[tile, window].astype(F32)).astype(BF)
+    def pull_back(query, keys, values, power, share, out, down):
+        scaled = down.astype(F32) * share
+        taken = (scaled * out.astype(F32)).astype(BF)
         scaled_rows = stack(scaled.astype(BF))
-        left = jnp.concatenate([scaled_rows, stack(-taken)], axis=1)
-        slope = nt(left, jnp.concatenate([values, ones], axis=1))
+        left_side = jnp.concatenate([scaled_rows, stack(-taken)], axis=1)
+        slope = nt(left_side, jnp.concatenate([values, ones], axis=1))
         slope = (power.astype(F32) * slope).astype(BF)
         side = jnp.concatenate([slope[128 * head : 128 * head + 128] for head in range(4)], axis=1)
-        pulled[2 * tiles + tile, window] = tn(power, scaled_rows).astype(BF)
-        pulled[tiles + tile, window] = (tn(slope, stack(query)) * SCALE).astype(BF)
-        pulled[tile, window] = (nn(side, stack(keys)) * SCALE).astype(BF)
+        return (
+            (nn(side, stack(keys)) * SCALE).astype(BF),
+            (tn(slope, stack(query)) * SCALE).astype(BF),
+            tn(power, scaled_rows).astype(BF),
+        )
+
+    def tile_step(step, carry):
+        pair = [((2 * step + side) // tiles, (2 * step + side) % tiles) for side in range(2)]
+        loaded = [
+            [qkv[part * tiles + tile, window] for part in range(3)]
+            + [raised[window, tile], inverse[window, tile], heads_out[tile, window], pulled[tile, window]]
+            for window, tile in pair
+        ]
+        made = [pull_back(*operands) for operands in loaded]
+        for (window, tile), grads in zip(pair, made):
+            for part in range(3):
+                pulled[part * tiles + tile, window] = grads[part]
         return carry
 
-    lax.fori_loop(0, windows * tiles, tile_step, 0)
+    lax.fori_loop(0, windows * tiles // 2, tile_step, 0)
     pulls = jnp.concatenate([pulled[tile].reshape(windows * 128, 128) for tile in range(3 * tiles)], axis=1)
     for step in range(tiles // 2):
         emit(slice(step * 256, step * 256 + 256), nt(pulls, weight_rows(w_qkv, shard, 3 * tiles, 256 * step, 256)))

time: 200 us -> 193 us (0.965)
  Pallas kernels: 191 us -> 184 us
    pallas_call x5, Pallas kernels: 191 us -> 184 us  [call(): pl.pallas_call(body, grid=(1,), out_shape=[jax.ShapeDtypeStruct(shape, ki...]
where the time goes in v2:
time: 193 us; the launch traced here: 190 us
  Pallas kernels  184 us (95%)
  local copies, waits for them, and re-layouts  3.03 us (2%)
  other arithmetic  2.12 us (1%)
    pallas_call x5, Pallas kernels, call(): pl.pallas_call(body, grid=(1,), out_shape=[jax.ShapeDtypeStruct(shape, ki...  184 us

profile of v2, /device:TPU:0, one launch (start us, length us, event | category | flops | bytes accessed | tf_op | source)
XLA Modules:
  0.0 190.2 jit_solution(16135103015686141579)
XLA Ops:
  0.6 0.7 slice.12
  1.3 0.9 pad_add_fusion
  2.2 0.9 fusion.1
  3.1 0.1 fusion.2
  3.2 0.1 copy.37
  3.3 0.1 copy.31
  3.4 0.1 reshape.73
  3.5 0.1 copy.32
  3.6 0.1 copy.33
  3.7 0.1 pad_add_fusion.1
  3.8 0.7 convert_element_type.18.refs_7_
  4.5 0.1 reshape.81
  4.6 0.2 reduce_max.9
  4.8 0.1 reshape.82
  4.9 0.1 copy.38
  5.0 0.1 copy.39
  5.1 0.1 pad_add_fusion.2
  5.2 0.7 convert_element_type.20.refs_15_
  5.8 49.7 %enter.1 = (bf16[8,4,32,512]{3,2,1,0:T(8,128)(2,1)}, bf16[8,32,512]{2,1,0:T(8,128)(2,1)}, bf16[4,32,512]{2,1,0:T(8,128)(2,1)}, bf16[1,32,512]{2,1,0:T(8,128)(2,1...) custom-call(bf16[3,12,24,512]{3,2,1,0:T(8,128)(2,1)} %bitcast.42, ...), custom_call_target="tpu_custom_call" | custom-call | flops 1000000000 | bytes 4194304 | tf_op jit(solution)/shard_map/enter/pallas_call | solution.py:661
  55.5 56.1 %first.1 = (bf16[8,4,32,512]{3,2,1,0:T(8,128)(2,1)}, bf16[8,32,512]{2,1,0:T(8,128)(2,1)}, bf16[4,32,512]{2,1,0:T(8,128)(2,1)}, bf16[1,32,512]{2,1,0:T(8,128)(2,1...) custom-call(bf16[8,4,32,512]{3,2,1,0:T(8,128)(2,1)} %get-tuple-eleme, ...), custom_call_target="tpu_custom_call", output_to_operand_aliasing={{9}: (9, {})} | custom-call | flops 1000000000 | bytes 4194304 | tf_op jit(solution)/shard_map/first/pallas_call | solution.py:661
  111.7 43.4 %middle.1 = (bf16[8,4,32,512]{3,2,1,0:T(8,128)(2,1)}, bf16[8,32,512]{2,1,0:T(8,128)(2,1)}, bf16[4,32,512]{2,1,0:T(8,128)(2,1)}, bf16[1,32,512]{2,1,0:T(8,128)(2,...) custom-call(bf16[8,4,32,512]{3,2,1,0:T(8,128)(2,1)} %get-tuple-eleme, ...), custom_call_target="tpu_custom_call" | custom-call | flops 1000000000 | bytes 4194304 | tf_op jit(solution)/shard_map/middle/pallas_call | solution.py:661
  155.1 30.6 %first_back.1 = (bf16[8,4,32,512]{3,2,1,0:T(8,128)(2,1)}, bf16[8,32,512]{2,1,0:T(8,128)(2,1)}, bf16[4,32,512]{2,1,0:T(8,128)(2,1)}, bf16[1,32,512]{2,1,0:T(8,128)(2,1)}) custom-call(bf16[8,4,32,512]{3,2,1,0:T(8,128)(2,1)} %get-tuple-element.51.refs_0_, bf16[8,32,512]{2,1,0:T(8,128)(2,1)} %get-tuple-element.52.refs_1_, ...), custom_call_target="tpu_custom_call" | custom-call | flops 1000000000 | bytes 4194304 | tf_op jit(solution)/shard_map/first_back/pallas_call | solution.py:661
  185.6 4.6 %leave.1 = (bf16[3,12,24,512]{3,2,1,0:T(8,128)(2,1)}, bf16[3,12,24,512]{3,2,1,0:T(8,128)(2,1)}) custom-call(bf16[8,4,32,512]{3,2,1,0:T(8,128)(2,1)} %get-tuple-element.60.own, bf16[8,32,512]{2,1,0:T(8,128)(2,1)} %get-tuple-element.61.lon, bf16[4,32,512]{2,1,0:T(8,128)(2,1)} %get-tuple-element.62.lat, bf16[1,32,512]{2,1,0:T(8,128)(2,1)} %get-tuple-element.63.diag, ...), custom_call_target="tpu_custom_call" | custom-call | flops 1000000000 | bytes 4194304 | tf_op jit(solution)/shard_map/leave/pallas_call | solution.py:661
  (4 shorter events, 0.0 us)
